TPU v7x, 32 devices: a whole 2x2x4 slice. The times are simulated.
32 devices in a mesh: expert: 8 (over z, core), tensor: 4 (over y, x).
Axes of the slice: x: 2, y: 2, z: 4, core: 2. Of those that a mesh axis runs over, the one named last changes fastest.
Arguments:
- grad_out: bfloat16 [4096, 2560], P(('expert', 'tensor')), may hold values from -6 to 6
- router_score: bfloat16 [4096], P(('expert', 'tensor')), may hold values from 0.19921875 to 1
- routing: int32 [4096, 1], P(('expert', 'tensor')), may hold values from 0 to 7; in each aligned block of 128 rows (0 to 127, 128 to 255, ...) at most 20 rows name the same one
- gate_pre: bfloat16 [8, 640, 4096], P('expert', None, 'tensor'), may hold values from -6 to 6
- up_pre: bfloat16 [8, 640, 4096], P('expert', None, 'tensor'), may hold values from -6 to 6
- gate_weight: bfloat16 [8, 2560, 4096], P('expert', None, 'tensor'), may hold values from -0.125 to 0.125
- up_weight: bfloat16 [8, 2560, 4096], P('expert', None, 'tensor'), may hold values from -0.125 to 0.125
- down_weight: bfloat16 [8, 4096, 2560], P('expert', 'tensor'), may hold values from -0.09375 to 0.09375
Outputs:
- grad_tokens: bfloat16 [4096, 2560], P(('expert', 'tensor'))
- grad_score: bfloat16 [4096], P(('expert', 'tensor'))
- grad_down_weight: bfloat16 [8, 4096, 2560], P('expert', 'tensor')
Inputs may be any that keep to these rules, and one draw needn't show every extreme that they name: `routing`: within the 128 rows of one device no expert is named by more than 20 rows, and in some device's rows one expert is named by exactly 20.
All inputs are finite; a program needn't handle non-finite values.
Results may differ from a plain program's by a relative error of at most 0.014.
Values may be sent and summed in bfloat16 or wider, within the bound.
A program may use at most 192 MiB of HBM per device.

v0:
```python
import jax
import jax.numpy as jnp
from jax import lax
from jax.sharding import PartitionSpec as P


def expert_rows(rows_grad, rows_score, gate_rows, up_rows, down_local):
    through = lax.dot_general(
        rows_grad, down_local, (((1,), (1,)), ((), ())), preferred_element_type=jnp.float32
    )
    gate_val = gate_rows.astype(jnp.float32)
    up_val = up_rows.astype(jnp.float32)
    sig_gate = jax.nn.sigmoid(gate_val)
    hidden = gate_val * sig_gate * up_val
    part_score = jnp.sum(through * hidden, axis=1)
    scale_col = rows_score.astype(jnp.float32)[:, None]
    scaled = scale_col * through
    grad_gate = (scaled * up_val * sig_gate * (1.0 + gate_val * (1.0 - sig_gate))).astype(
        jnp.bfloat16
    )
    grad_up = (scaled * gate_val * sig_gate).astype(jnp.bfloat16)
    weighted = (scale_col * hidden).astype(jnp.bfloat16)
    down_term = lax.dot_general(
        weighted, rows_grad, (((0,), (0,)), ((), ())), preferred_element_type=jnp.float32
    )
    return (grad_gate, grad_up, part_score, down_term)


def local(grad_out, router_score, routing, gate_pre, up_pre, gate_weight, up_weight, down_weight):
    n_expert = lax.axis_size("expert")
    tok_count = grad_out.shape[0]
    width = grad_out.shape[1]
    capacity = tok_count // n_expert + tok_count // (4 * n_expert)
    slot_count = n_expert * capacity
    gate_local = gate_pre[0]
    up_local = up_pre[0]
    down_local = down_weight[0]
    gate_mat = gate_weight[0]
    up_mat = up_weight[0]
    expert_ids = routing[:, 0]
    onehot = (expert_ids[:, None] == jnp.arange(n_expert, dtype=jnp.int32)[None, :]).astype(
        jnp.int32
    )
    before = jnp.cumsum(onehot, axis=0) - onehot
    position = jnp.sum(before * onehot, axis=1)
    slot_index = expert_ids * capacity + position
    send_grad = jnp.zeros((slot_count, width), jnp.bfloat16).at[slot_index].set(grad_out)
    send_score = jnp.zeros((slot_count,), jnp.bfloat16).at[slot_index].set(router_score)
    recv_grad, recv_score = (
        lax.all_to_all(
            send_grad.reshape(n_expert, capacity, width),
            "expert",
            split_axis=0,
            concat_axis=0,
            tiled=True,
        ),
        lax.all_to_all(
            send_score.reshape(n_expert, capacity),
            "expert",
            split_axis=0,
            concat_axis=0,
            tiled=True,
        ),
    )
    recv_grad = recv_grad.reshape(slot_count, width)
    recv_score = recv_score.reshape(slot_count)
    all_grad, all_score = (
        lax.all_gather(recv_grad, "tensor", axis=0, tiled=True),
        lax.all_gather(recv_score, "tensor", axis=0, tiled=True),
    )
    grad_gate, grad_up, part_score, down_sum = expert_rows(
        all_grad, all_score, gate_local, up_local, down_local
    )
    term = lax.dot_general(
        grad_gate, gate_mat, (((1,), (1,)), ((), ())), preferred_element_type=jnp.float32
    )
    mine_grad = lax.psum_scatter(
        (
            term
            + lax.dot_general(
                grad_up, up_mat, (((1,), (1,)), ((), ())), preferred_element_type=jnp.float32
            )
        ).astype(jnp.bfloat16),
        "tensor",
        scatter_dimension=0,
        tiled=True,
    )
    mine_score = lax.psum_scatter(part_score, "tensor", scatter_dimension=0, tiled=True)
    back_grad, back_score = (
        lax.all_to_all(
            mine_grad.reshape(n_expert, capacity, width),
            "expert",
            split_axis=0,
            concat_axis=0,
            tiled=True,
        ),
        lax.all_to_all(
            mine_score.astype(jnp.bfloat16).reshape(n_expert, capacity),
            "expert",
            split_axis=0,
            concat_axis=0,
            tiled=True,
        ),
    )
    grad_tokens = back_grad.reshape(slot_count, width)[slot_index]
    grad_score = back_score.reshape(slot_count)[slot_index]
    grad_down_weight = down_sum.astype(jnp.bfloat16)[None]
    return (grad_tokens, grad_score, grad_down_weight)


def solution(mesh):
    return jax.shard_map(
        local,
        mesh=mesh,
        in_specs=(
            P(("expert", "tensor"), None),
            P(("expert", "tensor")),
            P(("expert", "tensor"), None),
            P("expert", None, "tensor"),
            P("expert", None, "tensor"),
            P("expert", None, "tensor"),
            P("expert", None, "tensor"),
            P("expert", "tensor", None),
        ),
        out_specs=(
            P(("expert", "tensor"), None),
            P(("expert", "tensor")),
            P("expert", "tensor", None),
        ),
        check_vma=False,
    )
```

profile of v0, /device:TPU:0, one launch (start us, length us, event | category | flops | bytes accessed | tf_op | source)
XLA Modules:
  0.0 198.0 jit_solution(17634414762019741684)
XLA Ops:
  7.2 0.7 fusion.30
  8.0 0.2 reduce_window_sum.11
  8.1 0.8 select_reduce_fusion
  9.0 0.7 fusion.31
  9.6 2.3 %scatter_custom_fusion.1 = bf16[160,2560]{1,0:T(8,128)(2,1)S(1)} fusion(s32[128]{0:T(128)S(1)} %fusion.31, bf16[128,2560]{1,0:T(8,128)(2,1)} %param.8, bf16[]{:T(256)} %constant.6.clone.1), kind=kCustom, calls=%fused_computation.38 | custom fusion | bytes 819712 | tf_op jit(solution)/shard_map/scatter | solution.py:47
  11.9 0.2 reshape.41
  12.1 31.4 %all_to_all.30 = bf16[8,20,2560]{2,1,0:T(8,128)(2,1)S(1)} all-to-all(bf16[8,20,2560]{2,1,0:T(8,128)(2,1)S(1)} %reshape.41), channel_id=1, replica_groups=mesh['expert'=8,'tensor'=4] {'expert'}, dimensions={0} | all-to-all | bytes 1638400 | tf_op jit(solution)/shard_map/all_to_all | solution.py:50
  43.6 1.1 reshape.42
  44.7 1.5 scatter_custom_fusion
  46.2 0.7 all_to_all.24
  46.8 3.3 %all-to-all-start = ((bf16[8,1,20]{2,1,0:T(2,128)(2,1)}), bf16[8,1,20]{2,1,0:T(2,128)(2,1)S(1)}, u32[]{:S(2)}, u32[]{:S(2)}) async-start(bf16[8,1,20]{2,1,0:T(2,128)(2,1)} %all_to_all.24), calls=%async_computation | async-start | bytes 8192 | tf_op jit(solution)/shard_map/all_to_all | solution.py:57
  50.2 0.6 fusion.37
  51.4 4.2 %all-to-all-done = bf16[8,1,20]{2,1,0:T(2,128)(2,1)S(1)} async-done(((bf16[8,1,20]{2,1,0:T(2,128)(2,1)}), bf16[8,1,20]{2,1,0:T(2,128)(2,1)S(1)}, u32[]{:S(2)}, u32[]{:S(2)}) %all-to-all-start) | async-done | bytes 352 | tf_op jit(solution)/shard_map/all_to_all | solution.py:57
  55.6 0.1 reshape.80
  55.7 0.2 dynamic-update-slice
  55.9 10.0 %all-reduce = bf16[640]{0:T(1024)(128)(2,1)S(1)} all-reduce(bf16[640]{0:T(1024)(128)(2,1)S(1)} %dynamic-update-slice), channel_id=1, replica_groups=mesh['expert'=8,'tensor'=4] {'tensor'}, use_global_device_ids=true, to_apply=%add | all-reduce | flops 640 | bytes 2560
  65.9 23.0 %all-gather.2.cloned.1.call-done = bf16[640,2560]{1,0:T(8,128)(2,1)} async-done(((bf16[160,2560]{1,0:T(8,128)(2,1)}), bf16[640,2560]{1,0:T(8,128)(2,1)}) %all-gather.2.cloned.1.call-update) | async-done | bytes 3276816 | tf_op jit(solution)/shard_map/all_gather | solution.py:68
  88.9 7.7 %multiply_reduce_fusion = (f32[640]{0:T(1024)S(1)}, f32[640,1024]{1,0:T(8,128)S(1)}) fusion(bf16[1,640,1024]{2,1,0:T(8,128)(2,1)S(1)} %copy-done.1, bf16[1,640,1024]{2,1,0:T(8,128)(2,1)} %param.11, bf16[640,2560]{1,0:T(8,128)(2,1)} %all-gather.2.cloned.1.call-done, bf16[1,1024,2560]{2,1,0:T(8,128)(2,1)} %param.15), kind=kOutput, calls=%fused_computation.29 | convolution fusion | flops 3361340928 | bytes 13765120 | tf_op jit(solution)/shard_map/dot_general | solution.py:8
  96.6 6.6 %fusion = f32[640,2560]{1,0:T(8,128)S(1)} fusion(bf16[1,2560,1024]{2,1,0:T(8,128)(2,1)} %param.14, f32[640,1024]{1,0:T(8,128)S(1)} %get-tuple-element.6, bf16[1,640,1024]{2,1,0:T(8,128)(2,1)S(1)} %copy-done.2, f32[640]{0:T(1024)S(1)} %convert_element_type.37), kind=kOutput, calls=%fused_computation.6 | convolution fusion | flops 3360686080 | bytes 15731200 | tf_op jit(solution)/shard_map/dot_general | solution.py:80
  103.2 8.8 %add_convert_fusion = bf16[640,2560]{1,0:T(8,128)(2,1)} fusion(f32[640,2560]{1,0:T(8,128)S(1)} %fusion, bf16[1,2560,1024]{2,1,0:T(8,128)(2,1)} %param.13, f32[640,1024]{1,0:T(8,128)S(1)} %get-tuple-element.6, bf16[1,640,1024]{2,1,0:T(8,128)(2,1)S(1)} %copy-done.1, bf16[1,640,1024]{2,1,0:T(8,128)(2,1)S(1)} %copy-done.2, f32[640]{0:T(1024)S(1)} %convert_element_type.37), kind=kOutput, calls=%fused_computation.4 | convolution fusion | flops 3367239680 | bytes 20318720 | tf_op jit(solution)/shard_map/dot_general | solution.py:74
  112.7 9.1 %all-reduce.1 = bf16[640]{0:T(1024)(128)(2,1)S(1)} all-reduce(f32[640]{0:T(1024)S(1)} %get-tuple-element.5), channel_id=3, replica_groups=mesh['expert'=8,'tensor'=4] {'tensor'}, use_global_device_ids=true, to_apply=%region_6.7.clone | all-reduce | flops 640 | bytes 3840
  121.8 0.7 all_to_all.25
  122.5 4.6 %all-to-all-start.3 = ((bf16[8,1,20]{2,1,0:T(2,128)(2,1)}), bf16[8,1,20]{2,1,0:T(2,128)(2,1)S(1)}, u32[]{:S(2)}, u32[]{:S(2)}) async-start(bf16[8,1,20]{2,1,0:T(2,128)(2,1)} %all_to_all.25), calls=%async_computation.4 | async-start | bytes 8192 | tf_op jit(solution)/shard_map/all_to_all | solution.py:97
  127.1 30.1 %reduce-scatter.2.cloned.1.call-done = bf16[160,2560]{1,0:T(8,128)(2,1)} async-done(((bf16[640,2560]{1,0:T(8,128)(2,1)}), bf16[160,2560]{1,0:T(8,128)(2,1)}) %reduce-scatter.2.cloned.1.call-update) | async-done | bytes 819216 | tf_op jit(solution)/shard_map/reduce_scatter | solution.py:77
  157.2 2.2 %reshape.43 = bf16[8,20,2560]{2,1,0:T(8,128)(2,1)} reshape(bf16[160,2560]{1,0:T(8,128)(2,1)} %reduce-scatter.2.cloned.1.call-done) | data formatting | bytes 1638400 | tf_op jit(solution)/shard_map/reshape | solution.py:91
  159.4 4.6 %all-to-all-start.2 = ((bf16[8,20,2560]{2,1,0:T(8,128)(2,1)}), bf16[8,20,2560]{2,1,0:T(8,128)(2,1)S(1)}, u32[]{:S(2)}, u32[]{:S(2)}) async-start(bf16[8,20,2560]{2,1,0:T(8,128)(2,1)} %reshape.43), calls=%async_computation.3 | async-start | bytes 1966080 | tf_op jit(solution)/shard_map/all_to_all | solution.py:90
  164.0 9.4 %fusion.6 = bf16[1,1024,2560]{2,1,0:T(8,128)(2,1)} fusion(bf16[640,2560]{1,0:T(8,128)(2,1)} %all-gather.2.cloned.1.call-done, f32[640]{0:T(1024)S(1)} %convert_element_type.37, bf16[1,640,1024]{2,1,0:T(8,128)(2,1)S(1)} %copy-done.1, bf16[1,640,1024]{2,1,0:T(8,128)(2,1)} %param.11), kind=kOutput, calls=%fused_computation.12 | convolution fusion | flops 3363962880 | bytes 11143680 | tf_op jit(solution)/shard_map/dot_general | solution.py:23
  173.4 0.1 reshape.45
  173.5 1.7 gather_fusion.1
  175.2 14.0 %all-to-all-done.2 = bf16[8,20,2560]{2,1,0:T(8,128)(2,1)S(1)} async-done(((bf16[8,20,2560]{2,1,0:T(8,128)(2,1)}), bf16[8,20,2560]{2,1,0:T(8,128)(2,1)S(1)}, u32[]{:S(2)}, u32[]{:S(2)}) %all-to-all-start.2) | async-done | bytes 819232 | tf_op jit(solution)/shard_map/all_to_all | solution.py:90
  189.2 0.2 reshape.44
  189.4 1.8 gather_fusion
  (17 shorter events, 0.3 us)
Async XLA Ops:
  7.2 81.7 %all-gather.2.cloned.1.call-start = ((), (), s32[]{:S(2)}) async-start(), calls=%async_computation.5 | async-start | bytes 4096000 | tf_op jit(solution)/shard_map/all_gather | solution.py:68
  12.1 38.1 %copy-start = (u32[32]{0:T(128)S(1)}, u32[32]{0:T(128)}, u32[]{:S(2)}) copy-start(u32[32]{0:T(128)} %constant.25) | copy-start | bytes 388
  12.1 76.8 %copy-start.1 = (bf16[1,640,1024]{2,1,0:T(8,128)(2,1)S(1)}, bf16[1,640,1024]{2,1,0:T(8,128)(2,1)}, u32[]{:S(2)}) copy-start(bf16[1,640,1024]{2,1,0:T(8,128)(2,1)} %param.12) | copy-start | bytes 3932164
  46.8 8.7 %all-to-all-start = ((bf16[8,1,20]{2,1,0:T(2,128)(2,1)}), bf16[8,1,20]{2,1,0:T(2,128)(2,1)S(1)}, u32[]{:S(2)}, u32[]{:S(2)}) async-start(bf16[8,1,20]{2,1,0:T(2,128)(2,1)} %all_to_all.24), calls=%async_computation | async-start | bytes 8192 | tf_op jit(solution)/shard_map/all_to_all | solution.py:57
  50.2 107.1 %reduce-scatter.2.cloned.1.call-start = ((), (), s32[]{:S(2)}) async-start(), calls=%async_computation.6 | async-start | bytes 4096000 | tf_op jit(solution)/shard_map/reduce_scatter | solution.py:77
  65.9 30.7 %copy-start.2 = (bf16[1,640,1024]{2,1,0:T(8,128)(2,1)S(1)}, bf16[1,640,1024]{2,1,0:T(8,128)(2,1)}, u32[]{:S(2)}) copy-start(bf16[1,640,1024]{2,1,0:T(8,128)(2,1)} %param.11) | copy-start | bytes 3932164
  122.5 36.9 %all-to-all-start.3 = ((bf16[8,1,20]{2,1,0:T(2,128)(2,1)}), bf16[8,1,20]{2,1,0:T(2,128)(2,1)S(1)}, u32[]{:S(2)}, u32[]{:S(2)}) async-start(bf16[8,1,20]{2,1,0:T(2,128)(2,1)} %all_to_all.25), calls=%async_computation.4 | async-start | bytes 8192 | tf_op jit(solution)/shard_map/all_to_all | solution.py:97
  159.4 29.8 %all-to-all-start.2 = ((bf16[8,20,2560]{2,1,0:T(8,128)(2,1)}), bf16[8,20,2560]{2,1,0:T(8,128)(2,1)S(1)}, u32[]{:S(2)}, u32[]{:S(2)}) async-start(bf16[8,20,2560]{2,1,0:T(8,128)(2,1)} %reshape.43), calls=%async_computation.3 | async-start | bytes 1966080 | tf_op jit(solution)/shard_map/all_to_all | solution.py:90
Sparse Core Ops, SparseCore 0:
  44.8 44.0 all-gather.1
  112.1 45.0 reduce-scatter.1
where the time goes:
time: 199 us; the launch traced here: 198 us
  waiting for transfers between devices  71.3 us (36%)
  blocking collectives  50.5 us (25%)
  matrix products  32.4 us (16%)
  between operations  15.4 us (8%)
  local copies, waits for them, and re-layouts  13.4 us (7%)
  starting transfers between devices  12.6 us (6%)
  other arithmetic  2.46 us (1%)
    all_to_all x1, blocking collectives, local(): lax.all_to_all(send_grad.reshape(n_expert, capacity, width), 'expert', sp...  31.4 us
    reduce_scatter x1, waiting for transfers between devices, local(): lax.psum_scatter((term + lax.dot_general(grad_up, up_mat, (((1,), (1,)),...  30.1 us
    all_gather x1, waiting for transfers between devices, local(): lax.all_gather(recv_grad, 'tensor', axis=0, tiled=True)  23 us
    unnamed x2, blocking collectives  19.1 us
    all_to_all x1, waiting for transfers between devices, local(): lax.all_to_all(mine_grad.reshape(n_expert, capacity, width), 'expert', sp...  14 us
    dot_general x1, matrix products, expert_rows(): lax.dot_general(weighted, rows_grad, (((0,), (0,)), ((), ())), preferred_...  9.37 us
    dot_general x1, matrix products, local(): lax.dot_general(grad_gate, gate_mat, (((1,), (1,)), ((), ())), preferred_...  8.76 us
    dot_general x1, matrix products, expert_rows(): lax.dot_general(rows_grad, down_local, (((1,), (1,)), ((), ())), preferre...  7.72 us
  transfers between devices with their start and end apart: 5, of which 4 were waited for; matrix products, arithmetic and copies ran while one was open for 8% of the time, Pallas kernels for 0%

commit v1 on v0

--- a/solution.py
+++ b/solution.py
@@ -1,7 +1,536 @@
+import functools
+
 import jax
 import jax.numpy as jnp
 from jax import lax
+from jax.experimental import pallas as pl
+from jax.experimental.pallas import tpu as pltpu
 from jax.sharding import PartitionSpec as P
+
+MESH = pl.DeviceIdType.MESH
+LANES = 128
+PARTS = 4
+CHUNK = PARTS * LANES
+ROW_TILE = 16
+F32 = jnp.float32
+BF16 = jnp.bfloat16
+
+
+def dot_nn(a, b):
+    return lax.dot_general(a, b, (((1,), (0,)), ((), ())), preferred_element_type=F32)
+
+
+def dot_nt(a, b):
+    return lax.dot_general(a, b, (((1,), (1,)), ((), ())), preferred_element_type=F32)
+
+
+def dot_tn(a, b):
+    return lax.dot_general(a, b, (((0,), (0,)), ((), ())), preferred_element_type=F32)
+
+
+def split_bf16(value):
+    high = value.astype(BF16)
+    return high, (value - high.astype(F32)).astype(BF16)
+
+
+def iota(shape, dim):
+    return lax.broadcasted_iota(jnp.int32, shape, dim)
+
+
+def one_where(mask):
+    return jnp.where(mask, 1.0, 0.0).astype(BF16)
+
+
+def kernel(
+    n_expert, cap, n_chunk,
+    grad_ref, score_ref, routing_ref, gate_pre_ref, up_pre_ref, gate_w_ref, up_w_ref, down_w_ref,
+    tokens_ref, score_out_ref, down_out_ref,
+    gate_w, up_w, down_w, gate_v, up_v, coef_gate, coef_up, hidden, through, grad_gate, grad_up,
+    pick_send, pick_back, gather_mat, spread_mat,
+    send, recv, rows, term, got_first, sum_out, got_second, ret, back, down_part,
+    row_sum, score_part, score_got, score_tot, score_back,
+    z_send, z_recv, ag_send, ag_recv, first_send, first_recv, second_send, second_recv,
+    rz_send, rz_recv, sp_send, sp_recv, sz_send, sz_recv, load_sem, out_sem,
+):
+    tok = grad_ref.shape[0]
+    block = n_expert * cap
+    half = block // 2
+    piece = PARTS * cap
+    n_rows = PARTS * block
+    hid = gate_v.shape[1]
+    me_e = lax.axis_index("expert")
+    me_t = lax.axis_index("tensor")
+    tx = me_t + 1 - 2 * lax.rem(me_t, 2)
+    ty = lax.rem(me_t + 2, 4)
+    td = 3 - me_t
+    peers = (me_t, tx, ty, td)
+
+    barrier = pltpu.get_barrier_semaphore()
+    for d in range(1, n_expert):
+        pl.semaphore_signal(
+            barrier, inc=1, device_id=(lax.rem(me_e + d, n_expert), me_t), device_id_type=MESH
+        )
+    for j in range(1, 4):
+        pl.semaphore_signal(barrier, inc=1, device_id=(me_e, peers[j]), device_id_type=MESH)
+
+    loads = []
+    for j in range(4):
+        start = pl.multiple_of(peers[j] * block, block)
+        for k, (src, dst) in enumerate(((gate_pre_ref, gate_v), (up_pre_ref, up_v))):
+            loads.append(
+                pltpu.make_async_copy(
+                    src.at[0, pl.ds(start, block)],
+                    dst.at[pl.ds(j * block, block)],
+                    load_sem.at[2 * j + k],
+                )
+            )
+    load_down = pltpu.make_async_copy(down_w_ref.at[0], down_w, load_sem.at[8])
+    load_gate = pltpu.make_async_copy(gate_w_ref.at[0], gate_w, load_sem.at[9])
+    load_up = pltpu.make_async_copy(up_w_ref.at[0], up_w, load_sem.at[10])
+    for copy in loads + [load_down, load_gate, load_up]:
+        copy.start()
+
+    def remote(src, dst, s_sem, r_sem, e, t):
+        return pltpu.make_async_remote_copy(
+            src_ref=src, dst_ref=dst, send_sem=s_sem, recv_sem=r_sem,
+            device_id=(e, t), device_id_type=MESH,
+        )
+
+    routing = routing_ref[...]
+    named = iota((ROW_TILE, tok), 0) == routing
+    earlier = one_where(iota((tok, tok), 0) < iota((tok, tok), 1))
+    before = dot_nn(one_where(named), earlier)
+    place = jnp.sum(jnp.where(named, before, 0.0), axis=0, keepdims=True).astype(jnp.int32)
+    key = routing * piece + place
+    score = score_ref[...].astype(F32)
+    spot = iota((n_expert * piece, tok), 0)
+    for q in range(PARTS):
+        pick_send[:, q * tok : (q + 1) * tok] = jnp.where(
+            spot == key + q * cap, score, 0.0
+        ).astype(BF16)
+
+    def z_copy(c, d):
+        dest = lax.rem(me_e + d, n_expert)
+        return remote(
+            send.at[c, dest], recv.at[c, me_e], z_send.at[c, d], z_recv.at[c, d], dest, me_t
+        )
+
+    far_first = sorted(range(1, n_expert), key=lambda d: -min(d, n_expert - d))
+
+    for c in range(n_chunk):
+        stack = jnp.concatenate(
+            [
+                grad_ref[:, c * CHUNK + q * LANES : c * CHUNK + (q + 1) * LANES]
+                for q in range(PARTS)
+            ],
+            axis=0,
+        )
+        out = dot_nn(pick_send[...], stack).astype(BF16)
+        send[c] = out.reshape(n_expert, piece, LANES)
+        if c == 0:
+            pl.semaphore_wait(barrier, n_expert - 1 + 3)
+        for d in far_first:
+            z_copy(c, d).start()
+        recv[c, me_e] = send[c, me_e]
+
+    for q in range(PARTS):
+        r = iota((block, n_expert * piece), 0)
+        s = sum((r >= k * cap).astype(jnp.int32) for k in range(1, n_expert))
+        gather_mat[q * block : (q + 1) * block, :] = one_where(
+            iota((block, n_expert * piece), 1) == r + s * (piece - cap) + q * cap
+        )
+
+    def ag_copy(c, k):
+        if k == 0:
+            src, dst, t = rows.at[c, 0:block], rows.at[c, block : 2 * block], tx
+        elif k == 1:
+            src, dst, t = rows.at[c, 0:block], rows.at[c, 2 * block : 3 * block], ty
+        elif k == 2:
+            src, dst, t = (
+                rows.at[c, block : block + half], rows.at[c, 3 * block : 3 * block + half], ty
+            )
+        else:
+            src, dst, t = (
+                rows.at[c, 2 * block + half : 3 * block],
+                rows.at[c, 3 * block + half : 4 * block],
+                tx,
+            )
+        return remote(src, dst, ag_send.at[c, k], ag_recv.at[c, k], me_e, t)
+
+    def arrive(c):
+        for d in far_first[::-1]:
+            z_copy(c, d).wait_recv()
+        pieces = recv[c].reshape(n_expert * piece, LANES)
+        out = dot_nn(gather_mat[...], pieces).astype(BF16)
+        for q in range(PARTS):
+            rows[c, 0:block, q * LANES : (q + 1) * LANES] = out[q * block : (q + 1) * block]
+        ag_copy(c, 0).start()
+        ag_copy(c, 1).start()
+
+    def forward(c):
+        ag_copy(c, 0).wait_recv()
+        ag_copy(c, 2).start()
+        ag_copy(c, 1).wait_recv()
+        ag_copy(c, 3).start()
+
+    def through_part(c):
+        ag_copy(c, 2).wait_recv()
+        ag_copy(c, 3).wait_recv()
+
+        def body(j, carry):
+            at = pl.ds(pl.multiple_of(j * block, block), block)
+            part = dot_nt(rows[c, at, :], down_w[:, c * CHUNK : (c + 1) * CHUNK])
+            if c == 0:
+                through[at, :] = part
+            else:
+                through[at, :] = through[at, :] + part
+            return carry
+
+        lax.fori_loop(0, 4, body, 0)
+
+    def down_copy(c):
+        return pltpu.make_async_copy(
+            down_part.at[c], down_out_ref.at[0, :, c * CHUNK : (c + 1) * CHUNK], out_sem.at[c]
+        )
+
+    def down_term(c):
+        def body(i, carry):
+            at = pl.ds(pl.multiple_of(i * 256, 256), 256)
+            down_part[c, at, :] = dot_tn(hidden[:, at], rows[c]).astype(BF16)
+            return carry
+
+        lax.fori_loop(0, hid // 256, body, 0)
+        down_copy(c).start()
+
+    def coefficients():
+        for copy in loads:
+            copy.wait()
+
+        def body(i, carry):
+            at = pl.ds(pl.multiple_of(i * ROW_TILE, ROW_TILE), ROW_TILE)
+            gate = gate_v[at, :].astype(F32)
+            up = up_v[at, :].astype(F32)
+            sig = lax.logistic(gate)
+            silu = gate * sig
+            coef_up[at, :] = silu
+            coef_gate[at, :] = up * sig * (1.0 + gate * (1.0 - sig))
+            hidden[at, :] = (silu * up).astype(BF16)
+            return carry
+
+        lax.fori_loop(0, n_rows // ROW_TILE, body, 0)
+
+    arrive(0)
+    arrive(1)
+    coefficients()
+    forward(0)
+    arrive(2)
+    load_down.wait()
+    forward(1)
+    through_part(0)
+    arrive(3)
+    forward(2)
+    through_part(1)
+    arrive(4)
+    forward(3)
+    y = iota((n_expert * piece, PARTS * block), 1)
+    q_of = sum((y >= k * block).astype(jnp.int32) for k in range(1, PARTS))
+    r_of = y - q_of * block
+    s_of = sum((r_of >= k * cap).astype(jnp.int32) for k in range(1, n_expert))
+    spread_mat[...] = one_where(
+        iota((n_expert * piece, PARTS * block), 0) == r_of + s_of * (piece - cap) + q_of * cap
+    )
+    key_f = key.astype(F32)
+    key_col = jnp.sum(
+        jnp.where(iota((tok, tok), 0) == iota((tok, tok), 1), key_f, 0.0), axis=1, keepdims=True
+    ).astype(jnp.int32)
+    lane_spot = iota((tok, n_expert * piece), 1)
+    for q in range(PARTS):
+        pick_back[q * tok : (q + 1) * tok, :] = one_where(lane_spot == key_col + q * cap)
+    through_part(2)
+    forward(4)
+    down_term(0)
+    through_part(3)
+    down_term(1)
+    load_gate.wait()
+    load_up.wait()
+    through_part(4)
+
+    def grads(i, carry):
+        at = pl.ds(pl.multiple_of(i * ROW_TILE, ROW_TILE), ROW_TILE)
+        value = through[at, :]
+        silu = coef_up[at, :]
+        grad_gate[at, :] = (value * coef_gate[at, :]).astype(BF16)
+        grad_up[at, :] = (value * silu).astype(BF16)
+        prod = value * silu * up_v[at, :].astype(F32)
+        total = prod[:, 0:LANES]
+        for k in range(1, hid // LANES):
+            total = total + prod[:, k * LANES : (k + 1) * LANES]
+        row_sum[at, :] = total
+        return carry
+
+    lax.fori_loop(0, n_rows // ROW_TILE, grads, 0)
+
+    def first_copy(c, k):
+        begin = ((block, tx), (3 * block, tx), (2 * block + half, ty), (3 * block + half, ty))[k]
+        return remote(
+            term.at[c, begin[0] : begin[0] + half], got_first.at[c, k],
+            first_send.at[c, k], first_recv.at[c, k], me_e, begin[1],
+        )
+
+    def second_copy(c, k):
+        return remote(
+            sum_out.at[c, k], got_second.at[c, k],
+            second_send.at[c, k], second_recv.at[c, k], me_e, (ty, tx)[k],
+        )
+
+    def rz_copy(c, d):
+        dest = lax.rem(me_e + d, n_expert)
+        return remote(
+            ret.at[c, dest], back.at[c, me_e], rz_send.at[c, d], rz_recv.at[c, d], dest, me_t
+        )
+
+    def make_term(c):
+        gate_c = gate_w.at[c * CHUNK : (c + 1) * CHUNK, :]
+        up_c = up_w.at[c * CHUNK : (c + 1) * CHUNK, :]
+
+        def body(j, carry):
+            at = pl.ds(pl.multiple_of(j * block, block), block)
+            value = dot_nt(grad_gate[at, :], gate_c[...]) + dot_nt(grad_up[at, :], up_c[...])
+            term[c, at, :] = value.astype(BF16)
+            return carry
+
+        lax.fori_loop(0, 4, body, 0)
+        for k in range(4):
+            first_copy(c, k).start()
+
+    def add(a, b):
+        return a.astype(F32) + b.astype(F32)
+
+    def second_stage(c):
+        for k in range(2):
+            first_copy(c, k).wait_recv()
+        sum_out[c, 0] = add(term[c, 2 * block : 2 * block + half], got_first[c, 1]).astype(BF16)
+        second_copy(c, 0).start()
+        for k in range(2, 4):
+            first_copy(c, k).wait_recv()
+        sum_out[c, 1] = add(term[c, block + half : 2 * block], got_first[c, 3]).astype(BF16)
+        second_copy(c, 1).start()
+
+    def send_home(c):
+        second_copy(c, 0).wait_recv()
+        second_copy(c, 1).wait_recv()
+        low = add(term[c, 0:half], got_first[c, 0]) + got_second[c, 0].astype(F32)
+        high = add(term[c, half:block], got_first[c, 2]) + got_second[c, 1].astype(F32)
+        total = jnp.concatenate([low.astype(BF16), high.astype(BF16)], axis=0)
+        stack = jnp.concatenate(
+            [total[:, q * LANES : (q + 1) * LANES] for q in range(PARTS)], axis=0
+        )
+        out = dot_nn(spread_mat[...], stack).astype(BF16)
+        ret[c] = out.reshape(n_expert, piece, LANES)
+        for d in far_first:
+            rz_copy(c, d).start()
+        back[c, me_e] = ret[c, me_e]
+
+    def finish(c):
+        for d in far_first[::-1]:
+            rz_copy(c, d).wait_recv()
+        out = dot_nn(pick_back[...], back[c].reshape(n_expert * piece, LANES)).astype(BF16)
+        for q in range(PARTS):
+            tokens_ref[:, c * CHUNK + q * LANES : c * CHUNK + (q + 1) * LANES] = out[
+                q * tok : (q + 1) * tok
+            ]
+
+    wide = score_part.shape[2]
+
+    def sp_copy(j):
+        return remote(
+            score_part.at[j], score_got.at[j], sp_send.at[j], sp_recv.at[j], me_e, peers[j]
+        )
+
+    def sz_copy(d):
+        dest = lax.rem(me_e + d, n_expert)
+        return remote(
+            score_tot, score_back.at[me_e], sz_send.at[d], sz_recv.at[d], dest, me_t
+        )
+
+    def send_scores():
+        ones = jnp.ones((ROW_TILE, LANES), BF16)
+        score_part[...] = jnp.zeros(score_part.shape, F32)
+        for j in range(4):
+            high, low = split_bf16(row_sum[j * block : (j + 1) * block, :])
+            line = dot_nt(ones, high) + dot_nt(ones, low)
+            score_part[j, :, 0:block] = line[0:8]
+        for j in range(1, 4):
+            sp_copy(j).start()
+
+    def total_scores():
+        for j in range(1, 4):
+            sp_copy(j).wait_recv()
+        score_tot[...] = (score_part[0] + score_got[1]) + (score_got[2] + score_got[3])
+        for d in far_first:
+            sz_copy(d).start()
+        score_back[me_e] = score_tot[...]
+
+    def finish_scores():
+        for d in far_first:
+            sz_copy(d).wait_recv()
+        lane = iota((wide, tok), 0)
+        pick = one_where(lane == me_e * cap + place)
+        high, low = split_bf16(score_back[...].reshape(n_expert * 8, wide))
+        mixed = dot_nn(high, pick) + dot_nn(low, pick)
+        keep = iota((n_expert * 8, tok), 0) == routing * 8
+        value = jnp.sum(jnp.where(keep, mixed, 0.0), axis=0, keepdims=True)
+        score_out_ref[...] = (value / score).astype(BF16)
+
+    make_term(0)
+    make_term(1)
+    send_scores()
+    second_stage(0)
+    make_term(2)
+    second_stage(1)
+    send_home(0)
+    down_term(2)
+    make_term(3)
+    second_stage(2)
+    send_home(1)
+    total_scores()
+    make_term(4)
+    second_stage(3)
+    send_home(2)
+    finish(0)
+    down_term(3)
+    second_stage(4)
+    send_home(3)
+    finish(1)
+    down_term(4)
+    send_home(4)
+    finish(2)
+    finish_scores()
+    finish(3)
+    finish(4)
+
+    for c in range(n_chunk):
+        for d in range(1, n_expert):
+            z_copy(c, d).wait_send()
+            rz_copy(c, d).wait_send()
+        for k in range(4):
+            ag_copy(c, k).wait_send()
+            first_copy(c, k).wait_send()
+        for k in range(2):
+            second_copy(c, k).wait_send()
+        down_copy(c).wait()
+    for j in range(1, 4):
+        sp_copy(j).wait_send()
+    for d in range(1, n_expert):
+        sz_copy(d).wait_send()
+
+
+def fused_local(grad_out, router_score, routing, gate_pre, up_pre, gate_weight, up_weight, down_weight):
+    n_expert = lax.axis_size("expert")
+    tok, width = grad_out.shape
+    cap = tok // n_expert + tok // (4 * n_expert)
+    block = n_expert * cap
+    piece = PARTS * cap
+    n_rows = gate_pre.shape[1]
+    hid = gate_pre.shape[2]
+    n_chunk = width // CHUNK
+    wide = -(-block // LANES) * LANES
+    vmem = pl.BlockSpec(memory_space=pltpu.VMEM)
+    hbm = pl.BlockSpec(memory_space=pl.ANY)
+    dma = pltpu.SemaphoreType.DMA
+    macs = 4 * n_rows * width * hid
+    tokens, score, down = pl.pallas_call(
+        functools.partial(kernel, n_expert, cap, n_chunk),
+        out_shape=(
+            jax.ShapeDtypeStruct((tok, width), BF16),
+            jax.ShapeDtypeStruct((1, tok), BF16),
+            jax.ShapeDtypeStruct((1, hid, width), BF16),
+        ),
+        in_specs=[vmem, vmem, vmem, hbm, hbm, hbm, hbm, hbm],
+        out_specs=(vmem, vmem, hbm),
+        scratch_shapes=[
+            pltpu.VMEM((width, hid), BF16),
+            pltpu.VMEM((width, hid), BF16),
+            pltpu.VMEM((hid, width), BF16),
+            pltpu.VMEM((n_rows, hid), BF16),
+            pltpu.VMEM((n_rows, hid), BF16),
+            pltpu.VMEM((n_rows, hid), F32),
+            pltpu.VMEM((n_rows, hid), F32),
+            pltpu.VMEM((n_rows, hid), BF16),
+            pltpu.VMEM((n_rows, hid), F32),
+            pltpu.VMEM((n_rows, hid), BF16),
+            pltpu.VMEM((n_rows, hid), BF16),
+            pltpu.VMEM((n_expert * piece, PARTS * tok), BF16),
+            pltpu.VMEM((PARTS * tok, n_expert * piece), BF16),
+            pltpu.VMEM((PARTS * block, n_expert * piece), BF16),
+            pltpu.VMEM((n_expert * piece, PARTS * block), BF16),
+            pltpu.VMEM((n_chunk, n_expert, piece, LANES), BF16),
+            pltpu.VMEM((n_chunk, n_expert, piece, LANES), BF16),
+            pltpu.VMEM((n_chunk, n_rows, CHUNK), BF16),
+            pltpu.VMEM((n_chunk, n_rows, CHUNK), BF16),
+            pltpu.VMEM((n_chunk, 4, block // 2, CHUNK), BF16),
+            pltpu.VMEM((n_chunk, 2, block // 2, CHUNK), BF16),
+            pltpu.VMEM((n_chunk, 2, block // 2, CHUNK), BF16),
+            pltpu.VMEM((n_chunk, n_expert, piece, LANES), BF16),
+            pltpu.VMEM((n_chunk, n_expert, piece, LANES), BF16),
+            pltpu.VMEM((n_chunk, hid, CHUNK), BF16),
+            pltpu.VMEM((n_rows, LANES), F32),
+            pltpu.VMEM((4, 8, wide), F32),
+            pltpu.VMEM((4, 8, wide), F32),
+            pltpu.VMEM((8, wide), F32),
+            pltpu.VMEM((n_expert, 8, wide), F32),
+            dma((n_chunk, n_expert)),
+            dma((n_chunk, n_expert)),
+            dma((n_chunk, 4)),
+            dma((n_chunk, 4)),
+            dma((n_chunk, 4)),
+            dma((n_chunk, 4)),
+            dma((n_chunk, 2)),
+            dma((n_chunk, 2)),
+            dma((n_chunk, n_expert)),
+            dma((n_chunk, n_expert)),
+            dma((4,)),
+            dma((4,)),
+            dma((n_expert,)),
+            dma((n_expert,)),
+            dma((11,)),
+            dma((n_chunk,)),
+        ],
+        compiler_params=pltpu.CompilerParams(
+            collective_id=0, has_side_effects=True, vmem_limit_bytes=60 * 1024 * 1024
+        ),
+        cost_estimate=pl.CostEstimate(
+            flops=2 * macs,
+            bytes_accessed=2 * (4 * width * hid + 2 * n_rows * hid),
+            transcendentals=n_rows * hid,
+        ),
+        name="routed_backward",
+    )(
+        grad_out,
+        router_score.reshape(1, tok),
+        routing.reshape(1, tok),
+        gate_pre,
+        up_pre,
+        gate_weight,
+        up_weight,
+        down_weight,
+    )
+    return tokens, score.reshape(tok), down
+
+
+def fits(mesh, grad_out, gate_pre):
+    n_expert, n_tensor = mesh.shape["expert"], mesh.shape["tensor"]
+    tok = grad_out.shape[0] // (n_expert * n_tensor)
+    cap = tok // n_expert + tok // (4 * n_expert)
+    return (
+        n_tensor == 4
+        and n_expert <= ROW_TILE
+        and cap % 4 == 0
+        and (n_expert * cap) % 32 == 0
+        and tok % LANES == 0
+        and grad_out.shape[1] == 5 * CHUNK
+        and gate_pre.shape[2] % (256 * n_tensor) == 0
+    )
 
 
 def expert_rows(rows_grad, rows_score, gate_rows, up_rows, down_local):
@@ -109,23 +638,27 @@
 
 
 def solution(mesh):
-    return jax.shard_map(
-        local,
-        mesh=mesh,
-        in_specs=(
-            P(("expert", "tensor"), None),
-            P(("expert", "tensor")),
-            P(("expert", "tensor"), None),
-            P("expert", None, "tensor"),
-            P("expert", None, "tensor"),
-            P("expert", None, "tensor"),
-            P("expert", None, "tensor"),
-            P("expert", "tensor", None),
-        ),
-        out_specs=(
-            P(("expert", "tensor"), None),
-            P(("expert", "tensor")),
-            P("expert", "tensor", None),
-        ),
-        check_vma=False,
-    )
+    def run(*arrays):
+        body = fused_local if fits(mesh, arrays[0], arrays[3]) else local
+        return jax.shard_map(
+            body,
+            mesh=mesh,
+            in_specs=(
+                P(("expert", "tensor"), None),
+                P(("expert", "tensor")),
+                P(("expert", "tensor"), None),
+                P("expert", None, "tensor"),
+                P("expert", None, "tensor"),
+                P("expert", None, "tensor"),
+                P("expert", None, "tensor"),
+                P("expert", "tensor", None),
+            ),
+            out_specs=(
+                P(("expert", "tensor"), None),
+                P(("expert", "tensor")),
+                P("expert", "tensor", None),
+            ),
+            check_vma=False,
+        )(*arrays)
+
+    return run

time: 199 us -> 101 us (0.51)
  Pallas kernels: 0 us -> 92.1 us
  waiting for transfers between devices: 71.3 us -> 0 us
  blocking collectives: 50.5 us -> 0 us
  matrix products: 32.4 us -> 0 us
  between operations: 15.4 us -> 0.64 us
  starting transfers between devices: 12.6 us -> 0 us
  local copies, waits for them, and re-layouts: 13.4 us -> 8.27 us
  other arithmetic: 2.46 us -> 0 us
    pallas_call x0 -> x1, Pallas kernels: none -> 92.1 us  [fused_local(): pl.pallas_call(functools.partial(kernel, n_expert, cap, n_chunk), out_sha...]
    dot_general x4 -> x0, matrix products: 32.4 us -> none  [the longest x1 9.37 us: expert_rows(): lax.dot_general(weighted, rows_grad, (((0,), (0,)), ((), ())), preferred_...]
    all_to_all x1 -> x0, blocking collectives: 31.4 us -> none  [local(): lax.all_to_all(send_grad.reshape(n_expert, capacity, width), 'expert', sp...]
    reduce_scatter x1 -> x0, waiting for transfers between devices: 30.1 us -> none  [local(): lax.psum_scatter((term + lax.dot_general(grad_up, up_mat, (((1,), (1,)),...]
    all_gather x1 -> x0, waiting for transfers between devices: 23 us -> none  [local(): lax.all_gather(recv_grad, 'tensor', axis=0, tiled=True)]
    unnamed x2 -> x0, blocking collectives: 19.1 us -> none
    all_to_all x3 -> x0, waiting for transfers between devices: 18.2 us -> none  [the longest x1 14 us: local(): lax.all_to_all(mine_grad.reshape(n_expert, capacity, width), 'expert', sp...]
    all_to_all x3 -> x0, starting transfers between devices: 12.5 us -> none  [the longest x1 4.61 us: local(): lax.all_to_all(mine_grad.reshape(n_expert, capacity, width), 'expert', sp...]
  transfers between devices with their start and end apart: 5 -> 0, of which waited for: 4 -> 0; matrix products, arithmetic and copies ran while one was open for 8% -> 0% of each run, Pallas kernels for 0% -> 0%
where the time goes in v1:
time: 101 us
  Pallas kernels  92.1 us (91%)
  local copies, waits for them, and re-layouts  8.27 us (8%)
    pallas_call x1, Pallas kernels, fused_local(): pl.pallas_call(functools.partial(kernel, n_expert, cap, n_chunk), out_sha...  92.1 us
    unnamed x3, local copies, waits for them, and re-layouts  8.27 us

profile of v1, /device:TPU:0, one launch (start us, length us, event | category | flops | bytes accessed | tf_op | source)
XLA Modules:
  0.0 101.0 jit_solution(17023637769856977621)
XLA Ops:
  0.6 92.1 %routed_backward.1 = (bf16[128,2560]{1,0:T(8,128)(2,1)}, bf16[1,128]{1,0:T(2,128)(2,1)}, bf16[1,1024,2560]{2,1,0:T(8,128)(2,1)}) custom-call(bf16[128,2560]{1,0:T(8,128)(2,1)} %grad_ref.1, bf16[1,128]{1,0:T(2,128)(2,1)} %bitcast.3, s32[1,128]{1,0:T(1,128)} %bitcast.4, bf16[1,640,1024]{2,1,0:T(8,128)(2,1)} %gate_pre_ref.1, bf16[1,640,1024]{2,1,0:T(8,128)(2,1)} %up_pre_ref.1, ...), custom_call_target="tpu_custom_call" | custom-call | flops 13421772800 | bytes 23592960 | tf_op jit(solution)/shard_map/routed_backward/pallas_call | solution.py:442
  92.7 2.0 %copy.14 = bf16[128,2560]{1,0:T(8,128)(2,1)} copy(bf16[128,2560]{1,0:T(8,128)(2,1)} %get-tuple-element.12) | data formatting | bytes 1310720
  94.7 1.1 %copy.15 = bf16[128]{0:T(256)(128)(2,1)} copy(bf16[128]{0:T(256)(128)(2,1)} %bitcast.5) | data formatting | bytes 512
  95.8 5.2 %copy.16 = bf16[1,1024,2560]{2,1,0:T(8,128)(2,1)} copy(bf16[1,1024,2560]{2,1,0:T(8,128)(2,1)} %get-tuple-element.14) | data formatting | bytes 10485760

commit v2 on v1

--- a/solution.py
+++ b/solution.py
@@ -12,6 +12,7 @@
 PARTS = 4
 CHUNK = PARTS * LANES
 ROW_TILE = 16
+TILE = 256
 F32 = jnp.float32
 BF16 = jnp.bfloat16
 
@@ -45,12 +46,12 @@
     n_expert, cap, n_chunk,
     grad_ref, score_ref, routing_ref, gate_pre_ref, up_pre_ref, gate_w_ref, up_w_ref, down_w_ref,
     tokens_ref, score_out_ref, down_out_ref,
-    gate_w, up_w, down_w, gate_v, up_v, coef_gate, coef_up, hidden, through, grad_gate, grad_up,
+    gate_w, up_w, down_w, gate_v, up_v, coef_gate, coef_up, hidden_t, through, grad_gate, grad_up,
     pick_send, pick_back, gather_mat, spread_mat,
-    send, recv, rows, term, got_first, sum_out, got_second, ret, back, down_part,
+    send, recv, rows, term, got_first, sum_out, got_second, ret, back,
     row_sum, score_part, score_got, score_tot, score_back,
     z_send, z_recv, ag_send, ag_recv, first_send, first_recv, second_send, second_recv,
-    rz_send, rz_recv, sp_send, sp_recv, sz_send, sz_recv, load_sem, out_sem,
+    rz_send, rz_recv, sp_send, sp_recv, sz_send, sz_recv, load_sem,
 ):
     tok = grad_ref.shape[0]
     block = n_expert * cap
@@ -133,12 +134,20 @@
             z_copy(c, d).start()
         recv[c, me_e] = send[c, me_e]
 
+    key_f = key.astype(F32)
+    key_col = jnp.sum(
+        jnp.where(iota((tok, tok), 0) == iota((tok, tok), 1), key_f, 0.0), axis=1, keepdims=True
+    ).astype(jnp.int32)
+    lane_spot = iota((tok, n_expert * piece), 1)
+    for q in range(PARTS):
+        pick_back[q * tok : (q + 1) * tok, :] = one_where(lane_spot == key_col + q * cap)
     for q in range(PARTS):
         r = iota((block, n_expert * piece), 0)
         s = sum((r >= k * cap).astype(jnp.int32) for k in range(1, n_expert))
         gather_mat[q * block : (q + 1) * block, :] = one_where(
             iota((block, n_expert * piece), 1) == r + s * (piece - cap) + q * cap
         )
+    spread_mat[...] = gather_mat[...].T
 
     def ag_copy(c, k):
         if k == 0:
@@ -173,34 +182,32 @@
         ag_copy(c, 1).wait_recv()
         ag_copy(c, 3).start()
 
-    def through_part(c):
+    def wait_diagonal(c):
         ag_copy(c, 2).wait_recv()
         ag_copy(c, 3).wait_recv()
 
-        def body(j, carry):
-            at = pl.ds(pl.multiple_of(j * block, block), block)
-            part = dot_nt(rows[c, at, :], down_w[:, c * CHUNK : (c + 1) * CHUNK])
+    def through_part(c):
+        wait_diagonal(c)
+
+        def body(i, carry):
+            at = pl.ds(pl.multiple_of(i * TILE, TILE), TILE)
+            part = dot_nt(rows[c], down_w[at, c * CHUNK : (c + 1) * CHUNK])
             if c == 0:
-                through[at, :] = part
+                through[:, at] = part
             else:
-                through[at, :] = through[at, :] + part
+                through[:, at] = through[:, at] + part
             return carry
 
-        lax.fori_loop(0, 4, body, 0)
-
-    def down_copy(c):
-        return pltpu.make_async_copy(
-            down_part.at[c], down_out_ref.at[0, :, c * CHUNK : (c + 1) * CHUNK], out_sem.at[c]
-        )
+        lax.fori_loop(0, hid // TILE, body, 0)
 
     def down_term(c):
         def body(i, carry):
-            at = pl.ds(pl.multiple_of(i * 256, 256), 256)
-            down_part[c, at, :] = dot_tn(hidden[:, at], rows[c]).astype(BF16)
+            at = pl.ds(pl.multiple_of(i * TILE, TILE), TILE)
+            to = pl.ds(pl.multiple_of(c * CHUNK + i * TILE, TILE), TILE)
+            down_out_ref[0, :, to] = dot_nn(hidden_t[...], rows[c, :, at]).astype(BF16)
             return carry
 
-        lax.fori_loop(0, hid // 256, body, 0)
-        down_copy(c).start()
+        lax.fori_loop(0, CHUNK // TILE, body, 0)
 
     def coefficients():
         for copy in loads:
@@ -214,10 +221,17 @@
             silu = gate * sig
             coef_up[at, :] = silu
             coef_gate[at, :] = up * sig * (1.0 + gate * (1.0 - sig))
-            hidden[at, :] = (silu * up).astype(BF16)
+            grad_up[at, :] = (silu * up).astype(BF16)
             return carry
 
         lax.fori_loop(0, n_rows // ROW_TILE, body, 0)
+
+        def turn(i, carry):
+            at = pl.ds(pl.multiple_of(i * LANES, LANES), LANES)
+            hidden_t[:, at] = grad_up[at, :].T
+            return carry
+
+        lax.fori_loop(0, n_rows // LANES, turn, 0)
 
     arrive(0)
     arrive(1)
@@ -232,28 +246,10 @@
     through_part(1)
     arrive(4)
     forward(3)
-    y = iota((n_expert * piece, PARTS * block), 1)
-    q_of = sum((y >= k * block).astype(jnp.int32) for k in range(1, PARTS))
-    r_of = y - q_of * block
-    s_of = sum((r_of >= k * cap).astype(jnp.int32) for k in range(1, n_expert))
-    spread_mat[...] = one_where(
-        iota((n_expert * piece, PARTS * block), 0) == r_of + s_of * (piece - cap) + q_of * cap
-    )
-    key_f = key.astype(F32)
-    key_col = jnp.sum(
-        jnp.where(iota((tok, tok), 0) == iota((tok, tok), 1), key_f, 0.0), axis=1, keepdims=True
-    ).astype(jnp.int32)
-    lane_spot = iota((tok, n_expert * piece), 1)
-    for q in range(PARTS):
-        pick_back[q * tok : (q + 1) * tok, :] = one_where(lane_spot == key_col + q * cap)
     through_part(2)
-    forward(4)
-    down_term(0)
-    through_part(3)
-    down_term(1)
     load_gate.wait()
     load_up.wait()
-    through_part(4)
+    through_part(3)
 
     def grads(i, carry):
         at = pl.ds(pl.multiple_of(i * ROW_TILE, ROW_TILE), ROW_TILE)
@@ -268,7 +264,19 @@
         row_sum[at, :] = total
         return carry
 
-    lax.fori_loop(0, n_rows // ROW_TILE, grads, 0)
+    def finish_block(j):
+        last = n_chunk - 1
+        span = slice(j * block, (j + 1) * block)
+
+        def body(i, carry):
+            at = pl.ds(pl.multiple_of(i * TILE, TILE), TILE)
+            part = dot_nt(rows[last, span, :], down_w[at, last * CHUNK : (last + 1) * CHUNK])
+            through[span, at] = through[span, at] + part
+            return carry
+
+        lax.fori_loop(0, hid // TILE, body, 0)
+        per = block // ROW_TILE
+        lax.fori_loop(j * per, (j + 1) * per, grads, 0)
 
     def first_copy(c, k):
         begin = ((block, tx), (3 * block, tx), (2 * block + half, ty), (3 * block + half, ty))[k]
@@ -290,18 +298,31 @@
         )
 
     def make_term(c):
-        gate_c = gate_w.at[c * CHUNK : (c + 1) * CHUNK, :]
-        up_c = up_w.at[c * CHUNK : (c + 1) * CHUNK, :]
-
-        def body(j, carry):
-            at = pl.ds(pl.multiple_of(j * block, block), block)
-            value = dot_nt(grad_gate[at, :], gate_c[...]) + dot_nt(grad_up[at, :], up_c[...])
-            term[c, at, :] = value.astype(BF16)
-            return carry
-
-        lax.fori_loop(0, 4, body, 0)
+        for n in range(CHUNK // TILE):
+            at = slice(c * CHUNK + n * TILE, c * CHUNK + (n + 1) * TILE)
+
+            def body(j, carry):
+                span = pl.ds(pl.multiple_of(j * 2 * block, 2 * block), 2 * block)
+                value = dot_nt(grad_gate[span, :], gate_w[at, :])
+                value = value + dot_nt(grad_up[span, :], up_w[at, :])
+                term[c, span, n * TILE : (n + 1) * TILE] = value.astype(BF16)
+                return carry
+
+            lax.fori_loop(0, 2, body, 0)
         for k in range(4):
             first_copy(c, k).start()
+
+    def first_block(j):
+        span = slice(j * block, (j + 1) * block)
+
+        def body(i, carry):
+            at = pl.ds(pl.multiple_of(i * TILE, TILE), TILE)
+            value = dot_nt(grad_gate[span, :], gate_w[at, :])
+            value = value + dot_nt(grad_up[span, :], up_w[at, :])
+            term[0, span, at] = value.astype(BF16)
+            return carry
+
+        lax.fori_loop(0, CHUNK // TILE, body, 0)
 
     def add(a, b):
         return a.astype(F32) + b.astype(F32)
@@ -382,25 +403,40 @@
         value = jnp.sum(jnp.where(keep, mixed, 0.0), axis=0, keepdims=True)
         score_out_ref[...] = (value / score).astype(BF16)
 
-    make_term(0)
+    finish_block(0)
+    forward(n_chunk - 1)
+    finish_block(1)
+    first_block(1)
+    first_copy(0, 0).start()
+    finish_block(2)
+    first_block(2)
+    first_copy(0, 2).start()
+    wait_diagonal(n_chunk - 1)
+    finish_block(3)
+    first_block(3)
+    first_copy(0, 1).start()
+    first_copy(0, 3).start()
     make_term(1)
+    first_block(0)
     send_scores()
     second_stage(0)
     make_term(2)
     second_stage(1)
     send_home(0)
-    down_term(2)
+    down_term(0)
     make_term(3)
     second_stage(2)
     send_home(1)
+    down_term(1)
     total_scores()
     make_term(4)
     second_stage(3)
     send_home(2)
+    down_term(2)
+    second_stage(4)
+    send_home(3)
     finish(0)
     down_term(3)
-    second_stage(4)
-    send_home(3)
     finish(1)
     down_term(4)
     send_home(4)
@@ -418,11 +454,26 @@
             first_copy(c, k).wait_send()
         for k in range(2):
             second_copy(c, k).wait_send()
-        down_copy(c).wait()
     for j in range(1, 4):
         sp_copy(j).wait_send()
     for d in range(1, n_expert):
         sz_copy(d).wait_send()
+
+
+def hand_over(tokens_ref, score_ref, down_ref, tokens_out, score_out, down_out, out_sem):
+    n_part = out_sem.shape[0] - 2
+    height = down_ref.shape[1] // n_part
+    pairs = [
+        (down_ref.at[0, i * height : (i + 1) * height],
+         down_out.at[0, i * height : (i + 1) * height])
+        for i in range(n_part)
+    ]
+    pairs += [(tokens_ref, tokens_out), (score_ref, score_out)]
+    outs = [pltpu.make_async_copy(a, b, out_sem.at[i]) for i, (a, b) in enumerate(pairs)]
+    for out in outs:
+        out.start()
+    for out in outs:
+        out.wait()
 
 
 def fused_local(grad_out, router_score, routing, gate_pre, up_pre, gate_weight, up_weight, down_weight):
@@ -442,12 +493,12 @@
     tokens, score, down = pl.pallas_call(
         functools.partial(kernel, n_expert, cap, n_chunk),
         out_shape=(
-            jax.ShapeDtypeStruct((tok, width), BF16),
-            jax.ShapeDtypeStruct((1, tok), BF16),
-            jax.ShapeDtypeStruct((1, hid, width), BF16),
+            pltpu.VMEM((tok, width), BF16),
+            pltpu.VMEM((1, tok), BF16),
+            pltpu.VMEM((1, hid, width), BF16),
         ),
         in_specs=[vmem, vmem, vmem, hbm, hbm, hbm, hbm, hbm],
-        out_specs=(vmem, vmem, hbm),
+        out_specs=(vmem, vmem, vmem),
         scratch_shapes=[
             pltpu.VMEM((width, hid), BF16),
             pltpu.VMEM((width, hid), BF16),
@@ -456,7 +507,7 @@
             pltpu.VMEM((n_rows, hid), BF16),
             pltpu.VMEM((n_rows, hid), F32),
             pltpu.VMEM((n_rows, hid), F32),
-            pltpu.VMEM((n_rows, hid), BF16),
+            pltpu.VMEM((hid, n_rows), BF16),
             pltpu.VMEM((n_rows, hid), F32),
             pltpu.VMEM((n_rows, hid), BF16),
             pltpu.VMEM((n_rows, hid), BF16),
@@ -473,7 +524,6 @@
             pltpu.VMEM((n_chunk, 2, block // 2, CHUNK), BF16),
             pltpu.VMEM((n_chunk, n_expert, piece, LANES), BF16),
             pltpu.VMEM((n_chunk, n_expert, piece, LANES), BF16),
-            pltpu.VMEM((n_chunk, hid, CHUNK), BF16),
             pltpu.VMEM((n_rows, LANES), F32),
             pltpu.VMEM((4, 8, wide), F32),
             pltpu.VMEM((4, 8, wide), F32),
@@ -494,10 +544,9 @@
             dma((n_expert,)),
             dma((n_expert,)),
             dma((11,)),
-            dma((n_chunk,)),
         ],
         compiler_params=pltpu.CompilerParams(
-            collective_id=0, has_side_effects=True, vmem_limit_bytes=60 * 1024 * 1024
+            collective_id=0, has_side_effects=True, vmem_limit_bytes=54 * 1024 * 1024
         ),
         cost_estimate=pl.CostEstimate(
             flops=2 * macs,
@@ -515,6 +564,19 @@
         up_weight,
         down_weight,
     )
+    n_part = 4
+    tokens, score, down = pl.pallas_call(
+        hand_over,
+        out_shape=(
+            jax.ShapeDtypeStruct((tok, width), BF16),
+            jax.ShapeDtypeStruct((1, tok), BF16),
+            jax.ShapeDtypeStruct((1, hid, width), BF16),
+        ),
+        in_specs=[vmem, vmem, vmem],
+        out_specs=(hbm, hbm, hbm),
+        scratch_shapes=[dma((n_part + 2,))],
+        name="hand_over",
+    )(tokens, score, down)
     return tokens, score.reshape(tok), down
 
 

time: 101 us -> 98.9 us (0.979)
  local copies, waits for them, and re-layouts: 8.27 us -> 3.69 us
  Pallas kernels: 92.1 us -> 94.2 us
    pallas_call x0 -> x1, Pallas kernels: none -> 5.32 us  [fused_local(): pl.pallas_call(hand_over, out_shape=(jax.ShapeDtypeStruct((tok, width), B...]
    unnamed x3 -> x6, local copies, waits for them, and re-layouts: 8.27 us -> 3.69 us
    pallas_call x1, Pallas kernels: 92.1 us -> 88.9 us  [fused_local(): pl.pallas_call(functools.partial(kernel, n_expert, cap, n_chunk), out_sha...]
where the time goes in v2:
time: 98.9 us; the launch traced here: 98.7 us
  Pallas kernels  94.2 us (95%)
  local copies, waits for them, and re-layouts  3.69 us (4%)
    pallas_call x1, Pallas kernels, fused_local(): pl.pallas_call(functools.partial(kernel, n_expert, cap, n_chunk), out_sha...  88.9 us
    pallas_call x1, Pallas kernels, fused_local(): pl.pallas_call(hand_over, out_shape=(jax.ShapeDtypeStruct((tok, width), B...  5.32 us
    unnamed x6, local copies, waits for them, and re-layouts  3.69 us

profile of v2, /device:TPU:0, one launch (start us, length us, event | category | flops | bytes accessed | tf_op | source)
XLA Modules:
  0.0 98.7 jit_solution(4179714091743696564)
XLA Ops:
  0.6 88.9 %routed_backward.1 = (bf16[128,2560]{1,0:T(8,128)(2,1)S(1)}, bf16[1,128]{1,0:T(2,128)(2,1)S(1)}, bf16[1,1024,2560]{2,1,0:T(8,128)(2,1)S(1)}) custom-call(bf16[128,2560]{1,0:T(8,128)(2,1)} %grad_ref.1, bf16[1,128]{1,0:T(2,128)(2,1)} %bitcast.3, s32[1,128]{1,0:T(1,128)} %bitcast.4, bf16[1,640,1024]{2,1,0:T(8,128)(2,1)} %gate_pre_ref.1, ...), custom_call_target="tpu_custom_call" | custom-call | flops 13421772800 | bytes 23592960 | tf_op jit(solution)/shard_map/routed_backward/pallas_call | solution.py:493
  89.5 0.0 copy-start
  89.6 2.3 %copy-done = bf16[1,1024,2560]{2,1,0:T(8,128)(2,1)} copy-done((bf16[1,1024,2560]{2,1,0:T(8,128)(2,1)}, bf16[1,1024,2560]{2,1,0:T(8,128)(2,1)S(1)}, u32[]{:S(2)}) %copy-start) | copy-done | bytes 5242904
  91.8 0.0 copy-start.1
  91.8 0.9 copy-done.1
  92.7 0.0 copy-start.2
  92.7 0.5 copy-done.2
  93.2 5.3 %hand_over.1 = (bf16[128,2560]{1,0:T(8,128)(2,1)}, bf16[1,128]{1,0:T(2,128)(2,1)}, bf16[1,1024,2560]{2,1,0:T(8,128)(2,1)}) custom-call(bf16[128,2560]{1,0:T(8,128)(2,1)} %copy-done.1, bf16[1,128]{1,0:T(2,128)(2,1)} %copy-done.2, bf16[1,1024,2560]{2,1,0:T(8,128)(2,1)} %copy-done), custom_call_target="tpu_custom_call" | custom-call | tf_op jit(solution)/shard_map/hand_over/pallas_call | solution.py:568
Async XLA Ops:
  89.5 2.3 %copy-start = (bf16[1,1024,2560]{2,1,0:T(8,128)(2,1)}, bf16[1,1024,2560]{2,1,0:T(8,128)(2,1)S(1)}, u32[]{:S(2)}) copy-start(bf16[1,1024,2560]{2,1,0:T(8,128)(2,1)S(1)} %get-tuple-element.11.down_ref) | copy-start | bytes 15728644
  91.8 0.9 copy-start.1
  92.7 0.5 copy-start.2

commit v3 on v2

--- a/solution.py
+++ b/solution.py
@@ -61,9 +61,12 @@
     hid = gate_v.shape[1]
     me_e = lax.axis_index("expert")
     me_t = lax.axis_index("tensor")
-    tx = me_t + 1 - 2 * lax.rem(me_t, 2)
-    ty = lax.rem(me_t + 2, 4)
+    near = me_t + 1 - 2 * lax.rem(me_t, 2)
+    over = lax.rem(me_t + 2, 4)
     td = 3 - me_t
+    odd = lax.rem(me_e, 2)
+    tx = near + odd * (over - near)
+    ty = over + odd * (near - over)
     peers = (me_t, tx, ty, td)
 
     barrier = pltpu.get_barrier_semaphore()
@@ -118,7 +121,7 @@
 
     far_first = sorted(range(1, n_expert), key=lambda d: -min(d, n_expert - d))
 
-    for c in range(n_chunk):
+    def dispatch(c):
         stack = jnp.concatenate(
             [
                 grad_ref[:, c * CHUNK + q * LANES : c * CHUNK + (q + 1) * LANES]
@@ -133,6 +136,9 @@
         for d in far_first:
             z_copy(c, d).start()
         recv[c, me_e] = send[c, me_e]
+
+    dispatch(0)
+    dispatch(1)
 
     key_f = key.astype(F32)
     key_col = jnp.sum(
@@ -234,10 +240,13 @@
         lax.fori_loop(0, n_rows // LANES, turn, 0)
 
     arrive(0)
+    dispatch(2)
     arrive(1)
+    dispatch(3)
     coefficients()
     forward(0)
     arrive(2)
+    dispatch(4)
     load_down.wait()
     forward(1)
     through_part(0)
@@ -309,7 +318,7 @@
                 return carry
 
             lax.fori_loop(0, 2, body, 0)
-        for k in range(4):
+        for k in (0, 2, 1, 3):
             first_copy(c, k).start()
 
     def first_block(j):
@@ -575,6 +584,7 @@
         in_specs=[vmem, vmem, vmem],
         out_specs=(hbm, hbm, hbm),
         scratch_shapes=[dma((n_part + 2,))],
+        compiler_params=pltpu.CompilerParams(vmem_limit_bytes=1024 * 1024),
         name="hand_over",
     )(tokens, score, down)
     return tokens, score.reshape(tok), down

time: 98.9 us -> 90.8 us (0.918)
  Pallas kernels: 94.2 us -> 89.8 us
  local copies, waits for them, and re-layouts: 3.69 us -> 0 us
    unnamed x6 -> x0, local copies, waits for them, and re-layouts: 3.69 us -> none
    pallas_call x1, Pallas kernels: 5.32 us -> 2.62 us  [fused_local(): pl.pallas_call(hand_over, out_shape=(jax.ShapeDtypeStruct((tok, width), B...]
    pallas_call x1, Pallas kernels: 88.9 us -> 87.2 us  [fused_local(): pl.pallas_call(functools.partial(kernel, n_expert, cap, n_chunk), out_sha...]
where the time goes in v3:
time: 90.8 us; the launch traced here: 90.6 us
  Pallas kernels  89.8 us (99%)
    pallas_call x1, Pallas kernels, fused_local(): pl.pallas_call(functools.partial(kernel, n_expert, cap, n_chunk), out_sha...  87.2 us
    pallas_call x1, Pallas kernels, fused_local(): pl.pallas_call(hand_over, out_shape=(jax.ShapeDtypeStruct((tok, width), B...  2.62 us

profile of v3, /device:TPU:0, one launch (start us, length us, event | category | flops | bytes accessed | tf_op | source)
XLA Modules:
  0.0 90.6 jit_solution(2991706892239271269)
XLA Ops:
  0.6 87.2 %routed_backward.1 = (bf16[128,2560]{1,0:T(8,128)(2,1)S(1)}, bf16[1,128]{1,0:T(2,128)(2,1)S(1)}, bf16[1,1024,2560]{2,1,0:T(8,128)(2,1)S(1)}) custom-call(bf16[128,2560]{1,0:T(8,128)(2,1)} %grad_ref.1, bf16[1,128]{1,0:T(2,128)(2,1)} %bitcast.3, s32[1,128]{1,0:T(1,128)} %bitcast.4, bf16[1,640,1024]{2,1,0:T(8,128)(2,1)} %gate_pre_ref.1, ...), custom_call_target="tpu_custom_call" | custom-call | flops 13421772800 | bytes 23592960 | tf_op jit(solution)/shard_map/routed_backward/pallas_call | solution.py:502
  87.9 2.6 %hand_over.1 = (bf16[128,2560]{1,0:T(8,128)(2,1)}, bf16[1,128]{1,0:T(2,128)(2,1)}, bf16[1,1024,2560]{2,1,0:T(8,128)(2,1)}) custom-call(bf16[128,2560]{1,0:T(8,128)(2,1)S(1)} %get-tuple-element.9.tokens_ref, bf16[1,128]{1,0:T(2,128)(2,1)S(1)} %get-tuple-element.10.score_ref, bf16[1,1024,2560]{2,1,0:T(8,128)(2,1)S(1)} %get-tuple-element.11.down_ref), custom_call_target="tpu_custom_call" | custom-call | tf_op jit(solution)/shard_map/hand_over/pallas_call | solution.py:577

commit v4 on v3

--- a/solution.py
+++ b/solution.py
@@ -48,9 +48,9 @@
     tokens_ref, score_out_ref, down_out_ref,
     gate_w, up_w, down_w, gate_v, up_v, coef_gate, coef_up, hidden_t, through, grad_gate, grad_up,
     pick_send, pick_back, gather_mat, spread_mat,
-    send, recv, rows, term, got_first, sum_out, got_second, ret, back,
+    send, local_p, remote_p, rows, term, got_first, sum_out, got_second, ret, back,
     row_sum, score_part, score_got, score_tot, score_back,
-    z_send, z_recv, ag_send, ag_recv, first_send, first_recv, second_send, second_recv,
+    z_send, z_recv, lg_send, lg_recv, ag_send, ag_recv, first_send, first_recv, second_send, second_recv,
     rz_send, rz_recv, sp_send, sp_recv, sz_send, sz_recv, load_sem,
 ):
     tok = grad_ref.shape[0]
@@ -113,13 +113,24 @@
             spot == key + q * cap, score, 0.0
         ).astype(BF16)
 
-    def z_copy(c, d):
-        dest = lax.rem(me_e + d, n_expert)
+    plane = me_e // 2
+    core = lax.rem(me_e, 2)
+    n_plane = n_expert // 2
+
+    def z_copy(c, dz, dc):
+        dest = lax.rem(plane + dz, n_plane) * 2 + lax.rem(core + dc, 2)
+        seen = (n_plane - dz) % n_plane
+        if dz == 0:
+            landing = local_p.at[0, core, c]
+        else:
+            landing = remote_p.at[0, c, (seen - 1) * 2 + core]
         return remote(
-            send.at[c, dest], recv.at[c, me_e], z_send.at[c, d], z_recv.at[c, d], dest, me_t
+            send.at[c, dest], landing, z_send.at[c, 2 * dz + dc], z_recv.at[c, 2 * seen + dc],
+            dest, me_t,
         )
 
     far_first = sorted(range(1, n_expert), key=lambda d: -min(d, n_expert - d))
+    z_order = sorted(range(1, n_plane), key=lambda d: -min(d, n_plane - d))
 
     def dispatch(c):
         stack = jnp.concatenate(
@@ -133,12 +144,33 @@
         send[c] = out.reshape(n_expert, piece, LANES)
         if c == 0:
             pl.semaphore_wait(barrier, n_expert - 1 + 3)
-        for d in far_first:
-            z_copy(c, d).start()
-        recv[c, me_e] = send[c, me_e]
+        z_copy(c, 0, 1).start()
+        local_p[0, core, c] = send[c, me_e]
+
+    def send_far(c):
+        for dz in z_order:
+            z_copy(c, dz, 0).start()
+            z_copy(c, dz, 1).start()
+
+    def local_copy(k):
+        src, dst, t = (
+            (local_p.at[0], local_p.at[1], tx),
+            (local_p.at[0], local_p.at[2], ty),
+            (local_p.at[1, 0], local_p.at[3, 0], ty),
+            (local_p.at[2, 1], local_p.at[3, 1], tx),
+        )[k]
+        return remote(src, dst, lg_send.at[k], lg_recv.at[k], me_e, t)
 
     dispatch(0)
+    send_far(0)
     dispatch(1)
+    send_far(1)
+    for c in range(2, n_chunk):
+        dispatch(c)
+    for c in range(n_chunk):
+        z_copy(c, 0, 1).wait_recv()
+    local_copy(0).start()
+    local_copy(1).start()
 
     key_f = key.astype(F32)
     key_col = jnp.sum(
@@ -150,37 +182,51 @@
     for q in range(PARTS):
         r = iota((block, n_expert * piece), 0)
         s = sum((r >= k * cap).astype(jnp.int32) for k in range(1, n_expert))
-        gather_mat[q * block : (q + 1) * block, :] = one_where(
-            iota((block, n_expert * piece), 1) == r + s * (piece - cap) + q * cap
-        )
-    spread_mat[...] = gather_mat[...].T
+        lane = iota((block, n_expert * piece), 1)
+        at = slice(q * block, (q + 1) * block)
+        spot_abs = r + s * (piece - cap) + q * cap
+        spread_t = one_where(lane == spot_abs)
+        shift = spot_abs - 2 * piece * plane
+        shift = jnp.where(shift < 0, shift + n_expert * piece, shift)
+        spread_mat[:, at] = spread_t.T
+        gather_mat[at, :] = one_where(lane == shift)
 
     def ag_copy(c, k):
-        if k == 0:
-            src, dst, t = rows.at[c, 0:block], rows.at[c, block : 2 * block], tx
-        elif k == 1:
-            src, dst, t = rows.at[c, 0:block], rows.at[c, 2 * block : 3 * block], ty
-        elif k == 2:
-            src, dst, t = (
-                rows.at[c, block : block + half], rows.at[c, 3 * block : 3 * block + half], ty
-            )
-        else:
-            src, dst, t = (
-                rows.at[c, 2 * block + half : 3 * block],
-                rows.at[c, 3 * block + half : 4 * block],
-                tx,
-            )
+        n_far = n_expert - 2
+        low, high = slice(0, n_far // 2), slice(n_far // 2, n_far)
+        src, dst, t = (
+            (remote_p.at[0, c], remote_p.at[1, c], tx),
+            (remote_p.at[0, c], remote_p.at[2, c], ty),
+            (remote_p.at[1, c, low], remote_p.at[3, c, low], ty),
+            (remote_p.at[2, c, high], remote_p.at[3, c, high], tx),
+        )[k]
         return remote(src, dst, ag_send.at[c, k], ag_recv.at[c, k], me_e, t)
 
     def arrive(c):
-        for d in far_first[::-1]:
-            z_copy(c, d).wait_recv()
-        pieces = recv[c].reshape(n_expert * piece, LANES)
-        out = dot_nn(gather_mat[...], pieces).astype(BF16)
-        for q in range(PARTS):
-            rows[c, 0:block, q * LANES : (q + 1) * LANES] = out[q * block : (q + 1) * block]
+        for dz in z_order:
+            z_copy(c, dz, 0).wait_recv()
+            z_copy(c, dz, 1).wait_recv()
         ag_copy(c, 0).start()
         ag_copy(c, 1).start()
+
+    def local_forward():
+        local_copy(0).wait_recv()
+        local_copy(2).start()
+        local_copy(1).wait_recv()
+        local_copy(3).start()
+
+    def pieces_of(c, j):
+        far = remote_p[j, c].reshape((n_expert - 2) * piece, LANES)
+        return jnp.concatenate([local_p[j, 0, c], local_p[j, 1, c], far], axis=0)
+
+    def to_slots(c, blocks):
+        wide_in = jnp.concatenate([pieces_of(c, j) for j in blocks], axis=1)
+        out = dot_nn(gather_mat[...], wide_in).astype(BF16)
+        for i, j in enumerate(blocks):
+            for q in range(PARTS):
+                rows[c, j * block : (j + 1) * block, q * LANES : (q + 1) * LANES] = out[
+                    q * block : (q + 1) * block, i * LANES : (i + 1) * LANES
+                ]
 
     def forward(c):
         ag_copy(c, 0).wait_recv()
@@ -194,6 +240,7 @@
 
     def through_part(c):
         wait_diagonal(c)
+        to_slots(c, range(4))
 
         def body(i, carry):
             at = pl.ds(pl.multiple_of(i * TILE, TILE), TILE)
@@ -240,21 +287,26 @@
         lax.fori_loop(0, n_rows // LANES, turn, 0)
 
     arrive(0)
-    dispatch(2)
+    send_far(2)
+    coefficients()
+    local_forward()
     arrive(1)
-    dispatch(3)
-    coefficients()
+    send_far(3)
     forward(0)
     arrive(2)
-    dispatch(4)
+    send_far(4)
+    forward(1)
     load_down.wait()
-    forward(1)
+    local_copy(2).wait_recv()
+    local_copy(3).wait_recv()
     through_part(0)
     arrive(3)
     forward(2)
+    down_term(0)
     through_part(1)
     arrive(4)
     forward(3)
+    down_term(1)
     through_part(2)
     load_gate.wait()
     load_up.wait()
@@ -275,6 +327,7 @@
 
     def finish_block(j):
         last = n_chunk - 1
+        to_slots(last, [j])
         span = slice(j * block, (j + 1) * block)
 
         def body(i, carry):
@@ -432,37 +485,37 @@
     make_term(2)
     second_stage(1)
     send_home(0)
-    down_term(0)
     make_term(3)
     second_stage(2)
     send_home(1)
-    down_term(1)
     total_scores()
     make_term(4)
     second_stage(3)
     send_home(2)
     down_term(2)
+    finish(0)
     second_stage(4)
     send_home(3)
-    finish(0)
     down_term(3)
     finish(1)
+    send_home(4)
     down_term(4)
-    send_home(4)
+    finish_scores()
     finish(2)
-    finish_scores()
     finish(3)
     finish(4)
 
     for c in range(n_chunk):
         for d in range(1, n_expert):
-            z_copy(c, d).wait_send()
+            z_copy(c, d // 2, d % 2).wait_send()
             rz_copy(c, d).wait_send()
         for k in range(4):
             ag_copy(c, k).wait_send()
             first_copy(c, k).wait_send()
         for k in range(2):
             second_copy(c, k).wait_send()
+    for k in range(4):
+        local_copy(k).wait_send()
     for j in range(1, 4):
         sp_copy(j).wait_send()
     for d in range(1, n_expert):
@@ -525,7 +578,8 @@
             pltpu.VMEM((PARTS * block, n_expert * piece), BF16),
             pltpu.VMEM((n_expert * piece, PARTS * block), BF16),
             pltpu.VMEM((n_chunk, n_expert, piece, LANES), BF16),
-            pltpu.VMEM((n_chunk, n_expert, piece, LANES), BF16),
+            pltpu.VMEM((4, 2, n_chunk, piece, LANES), BF16),
+            pltpu.VMEM((4, n_chunk, n_expert - 2, piece, LANES), BF16),
             pltpu.VMEM((n_chunk, n_rows, CHUNK), BF16),
             pltpu.VMEM((n_chunk, n_rows, CHUNK), BF16),
             pltpu.VMEM((n_chunk, 4, block // 2, CHUNK), BF16),
@@ -540,6 +594,8 @@
             pltpu.VMEM((n_expert, 8, wide), F32),
             dma((n_chunk, n_expert)),
             dma((n_chunk, n_expert)),
+            dma((4,)),
+            dma((4,)),
             dma((n_chunk, 4)),
             dma((n_chunk, 4)),
             dma((n_chunk, 4)),
@@ -597,6 +653,8 @@
     return (
         n_tensor == 4
         and n_expert <= ROW_TILE
+        and n_expert % 2 == 0
+        and n_expert >= 4
         and cap % 4 == 0
         and (n_expert * cap) % 32 == 0
         and tok % LANES == 0

time: 90.8 us -> 88.1 us (0.970)
  Pallas kernels: 89.8 us -> 87.1 us
    pallas_call x1, Pallas kernels: 87.2 us -> 84.5 us  [fused_local(): pl.pallas_call(functools.partial(kernel, n_expert, cap, n_chunk), out_sha...]
where the time goes in v4:
time: 88.1 us; the launch traced here: 87.9 us
  Pallas kernels  87.1 us (99%)
    pallas_call x1, Pallas kernels, fused_local(): pl.pallas_call(functools.partial(kernel, n_expert, cap, n_chunk), out_sha...  84.5 us
    pallas_call x1, Pallas kernels, fused_local(): pl.pallas_call(hand_over, out_shape=(jax.ShapeDtypeStruct((tok, width), B...  2.62 us

profile of v4, /device:TPU:0, one launch (start us, length us, event | category | flops | bytes accessed | tf_op | source)
XLA Modules:
  0.0 87.9 jit_solution(2734362453078356803)
XLA Ops:
  0.6 84.5 %routed_backward.1 = (bf16[128,2560]{1,0:T(8,128)(2,1)S(1)}, bf16[1,128]{1,0:T(2,128)(2,1)S(1)}, bf16[1,1024,2560]{2,1,0:T(8,128)(2,1)S(1)}) custom-call(bf16[128,2560]{1,0:T(8,128)(2,1)} %grad_ref.1, bf16[1,128]{1,0:T(2,128)(2,1)} %bitcast.3, s32[1,128]{1,0:T(1,128)} %bitcast.4, bf16[1,640,1024]{2,1,0:T(8,128)(2,1)} %gate_pre_ref.1, ...), custom_call_target="tpu_custom_call" | custom-call | flops 13421772800 | bytes 23592960 | tf_op jit(solution)/shard_map/routed_backward/pallas_call | solution.py:555
  85.1 2.6 %hand_over.1 = (bf16[128,2560]{1,0:T(8,128)(2,1)}, bf16[1,128]{1,0:T(2,128)(2,1)}, bf16[1,1024,2560]{2,1,0:T(8,128)(2,1)}) custom-call(bf16[128,2560]{1,0:T(8,128)(2,1)S(1)} %get-tuple-element.9.tokens_ref, bf16[1,128]{1,0:T(2,128)(2,1)S(1)} %get-tuple-element.10.score_ref, bf16[1,1024,2560]{2,1,0:T(8,128)(2,1)S(1)} %get-tuple-element.11.down_ref), custom_call_target="tpu_custom_call" | custom-call | tf_op jit(solution)/shard_map/hand_over/pallas_call | solution.py:633

commit v5 on v4

--- a/solution.py
+++ b/solution.py
@@ -306,8 +306,8 @@
     through_part(1)
     arrive(4)
     forward(3)
-    down_term(1)
     through_part(2)
+    forward(n_chunk - 1)
     load_gate.wait()
     load_up.wait()
     through_part(3)
@@ -466,7 +466,6 @@
         score_out_ref[...] = (value / score).astype(BF16)
 
     finish_block(0)
-    forward(n_chunk - 1)
     finish_block(1)
     first_block(1)
     first_copy(0, 0).start()
@@ -488,6 +487,7 @@
     make_term(3)
     second_stage(2)
     send_home(1)
+    down_term(1)
     total_scores()
     make_term(4)
     second_stage(3)

time: 88.1 us -> 88.8 us (level)
  no operation moved by 1% of the time
where the time goes in v5:
time: 88.8 us; the launch traced here: 88.7 us
  Pallas kernels  87.8 us (99%)
    pallas_call x1, Pallas kernels, fused_local(): pl.pallas_call(functools.partial(kernel, n_expert, cap, n_chunk), out_sha...  85.2 us
    pallas_call x1, Pallas kernels, fused_local(): pl.pallas_call(hand_over, out_shape=(jax.ShapeDtypeStruct((tok, width), B...  2.62 us

profile of v5, /device:TPU:0, one launch (start us, length us, event | category | flops | bytes accessed | tf_op | source)
XLA Modules:
  0.0 88.7 jit_solution(15171333572322274255)
XLA Ops:
  0.6 85.2 %routed_backward.1 = (bf16[128,2560]{1,0:T(8,128)(2,1)S(1)}, bf16[1,128]{1,0:T(2,128)(2,1)S(1)}, bf16[1,1024,2560]{2,1,0:T(8,128)(2,1)S(1)}) custom-call(bf16[128,2560]{1,0:T(8,128)(2,1)} %grad_ref.1, bf16[1,128]{1,0:T(2,128)(2,1)} %bitcast.3, s32[1,128]{1,0:T(1,128)} %bitcast.4, bf16[1,640,1024]{2,1,0:T(8,128)(2,1)} %gate_pre_ref.1, ...), custom_call_target="tpu_custom_call" | custom-call | flops 13421772800 | bytes 23592960 | tf_op jit(solution)/shard_map/routed_backward/pallas_call | solution.py:555
  85.9 2.6 %hand_over.1 = (bf16[128,2560]{1,0:T(8,128)(2,1)}, bf16[1,128]{1,0:T(2,128)(2,1)}, bf16[1,1024,2560]{2,1,0:T(8,128)(2,1)}) custom-call(bf16[128,2560]{1,0:T(8,128)(2,1)S(1)} %get-tuple-element.9.tokens_ref, bf16[1,128]{1,0:T(2,128)(2,1)S(1)} %get-tuple-element.10.score_ref, bf16[1,1024,2560]{2,1,0:T(8,128)(2,1)S(1)} %get-tuple-element.11.down_ref), custom_call_target="tpu_custom_call" | custom-call | tf_op jit(solution)/shard_map/hand_over/pallas_call | solution.py:633
